TPU v7x, 256 devices: a whole 4x4x8 slice. The times are simulated.
256 devices in a mesh: dp: 4 (over x), vocab: 64 (over y, z, core).
Axes of the slice: x: 4, y: 4, z: 8, core: 2. Of those that a mesh axis runs over, the one named last changes fastest.
Arguments:
- features: bfloat16 [2048, 4096], P(('dp', 'vocab')), may hold values from -8 to 8
- head: bfloat16 [65536, 4096], P(('dp', 'vocab')), may hold values from -0.5 to 0.5
- momentum: bfloat16 [65536, 4096], P(('dp', 'vocab')), may hold values from -7.124618e-08 to 7.124618e-08
- hessian: bfloat16 [65536, 4096], P(('dp', 'vocab')), may hold values from 4.765752e-10 to 4.7683716e-06
- true_labels: int32 [2048], replicated, may hold values from 0 to 65535
- sampled_labels: int32 [2048], replicated, may hold values from 0 to 65535
Outputs:
- mean_loss: float32 [], replicated
- new_hessian: bfloat16 [65536, 4096], P(('dp', 'vocab'))
- update: bfloat16 [65536, 4096], P(('dp', 'vocab'))
All inputs are finite; a program needn't handle non-finite values.
Results may differ from a plain program's by a relative error of at most 0.019.
Values may be sent and summed in bfloat16 or wider, within the bound.
A program may use at most 128 MiB of HBM per device.

v0:
```python
import jax
import jax.numpy as jnp
from jax import lax
from jax.sharding import PartitionSpec as P

hess_decay = 0.99
clip_scale = 0.05


def local_stats(logits, columns, labels):
    highest = jnp.max(logits, axis=1)
    row_total = jnp.sum(jnp.exp(logits - highest[:, None]), axis=1)
    picked = jnp.sum(jnp.where(columns[None, :] == labels[:, None], logits, 0.0), axis=1)
    return (highest, row_total, picked)


def make_signal(logits, log_norm, columns, labels):
    chosen = (columns[None, :] == labels[:, None]).astype(jnp.float32)
    return (jnp.exp(logits - log_norm[:, None]) - chosen).astype(jnp.bfloat16)


def sophia_tail(gradient, momentum, hessian):
    fresh = hess_decay * hessian.astype(jnp.float32) + (1.0 - hess_decay) * gradient * gradient
    clipped = jnp.clip(momentum.astype(jnp.float32) / (clip_scale * fresh), -1.0, 1.0)
    return (fresh.astype(jnp.bfloat16), clipped.astype(jnp.bfloat16))


def shards(features, head, momentum, hessian, true_labels, sampled_labels):
    voc_dev = head.shape[0]
    every_row = lax.all_gather(features, ("dp", "vocab"), axis=0, tiled=True)
    logits = lax.dot_general(
        every_row, head, (((1,), (1,)), ((), ())), preferred_element_type=jnp.float32
    )
    own_offset = (lax.axis_index("dp") * lax.axis_size("vocab") + lax.axis_index("vocab")) * voc_dev
    columns = own_offset + jnp.arange(voc_dev, dtype=jnp.int32)
    highest, row_total, picked = local_stats(logits, columns, true_labels)
    top_all = lax.pmax(highest, ("dp", "vocab"))
    row_total, picked = lax.psum((row_total * jnp.exp(highest - top_all), picked), ("dp", "vocab"))
    highest = top_all
    log_norm = highest + jnp.log(row_total)
    mean_loss = jnp.mean(log_norm - picked)
    signal = make_signal(logits, log_norm, columns, sampled_labels)
    groups = lax.axis_size("dp")
    signal_groups = signal.reshape(groups, -1, voc_dev)
    row_groups = every_row.reshape(groups, -1, every_row.shape[1])
    partials = lax.dot_general(
        signal_groups, row_groups, (((1,), (1,)), ((0,), (0,))), preferred_element_type=jnp.float32
    )
    rounded = lax.optimization_barrier(partials.astype(jnp.bfloat16)).astype(jnp.float32)
    gradient = jnp.sum(rounded, axis=0)
    fresh, clipped = sophia_tail(gradient, momentum, hessian)
    return (mean_loss, fresh, clipped)


def solution(mesh):
    in_specs = (
        P(("dp", "vocab"), None),
        P(("dp", "vocab"), None),
        P(("dp", "vocab"), None),
        P(("dp", "vocab"), None),
        P(),
        P(),
    )
    out_specs = (P(), P(("dp", "vocab"), None), P(("dp", "vocab"), None))
    return jax.shard_map(shards, mesh=mesh, in_specs=in_specs, out_specs=out_specs, check_vma=False)
```

profile of v0, /device:TPU:1, one launch (start us, length us, event | category | flops | bytes accessed | tf_op | source)
XLA Modules:
  0.0 339.7 jit_solution(14028145733843676023)
XLA Ops:
  7.2 0.0 copy-start
  7.2 0.0 all-gather.2.cloned.1.call-start
  7.2 0.7 all-gather.2.cloned.1.call-update
  7.9 0.0 copy-start.1
  7.9 133.0 %all-gather.2.cloned.1.call-done = bf16[2048,4096]{1,0:T(8,128)(2,1)} async-done(((bf16[8,4096]{1,0:T(8,128)(2,1)}), bf16[2048,4096]{1,0:T(8,128)(2,1)}) %all-gather.2.cloned.1.call-update) | async-done | bytes 16777232 | tf_op jit(solution)/shard_map/all_gather | solution.py:30
  140.9 0.0 copy-done
  140.9 9.8 %fusion.2 = (f32[2048]{0:T(1024)S(1)}, f32[2048,256]{1,0:T(8,128)}) fusion(bf16[2048,4096]{1,0:T(8,128)(2,1)} %all-gather.2.cloned.1.call-done, bf16[256,4096]{1,0:T(8,128)(2,1)S(1)} %copy-done), kind=kOutput, calls=%fused_computation.13 | convolution fusion | flops 4295489536 | bytes 20979712 | tf_op jit(solution)/shard_map/dot_general | solution.py:31
  150.8 0.0 copy-start.2
  150.8 74.4 %pmax.7 = f32[2048]{0:T(1024)S(1)} all-reduce(f32[2048]{0:T(1024)S(1)} %get-tuple-element.11), channel_id=1, replica_groups=mesh['dp'=4,'vocab'=64] {'dp','vocab'}, use_global_device_ids=true, to_apply=%region_1.0 | all-reduce | flops 2048 | bytes 16384 | tf_op jit(solution)/shard_map/pmax | solution.py:37
  225.2 0.0 copy-done.1
  225.2 2.5 select_reduce_fusion
  227.7 73.8 %all-reduce = (f32[2048]{0:T(1024)S(1)}, f32[2048]{0:T(1024)S(1)}) all-reduce(f32[2048]{0:T(1024)S(1)} %exponential_multiply_fusion, f32[2048]{0:T(1024)S(1)} %get-tuple-element.3), channel_id=1, replica_groups=mesh['dp'=4,'vocab'=64] {'dp','vocab'}, use_global_device_ids=true, to_apply=%region_3.4 | all-reduce | flops 4096 | bytes 32768 | tf_op jit(solution)/shard_map/psum | solution.py:38
  301.5 0.6 subtract_reduce_fusion
  302.1 0.0 copy-done.2
  302.2 1.9 subtract_convert_fusion
  304.1 12.6 %convolution_convert_fusion = bf16[4,256,4096]{2,1,0:T(8,128)(2,1)} fusion(bf16[4,512,256]{2,1,0:T(8,128)(2,1)S(1)} %bitcast.7, bf16[4,512,4096]{2,1,0:T(8,128)(2,1)} %bitcast.6), kind=kOutput, calls=%fused_computation.1 | convolution fusion | flops 4299161600 | bytes 26214400 | tf_op jit(solution)/shard_map/dot_general | solution.py:46
  316.7 7.3 %convert_reduce_fusion = f32[256,4096]{1,0:T(8,128)} fusion(bf16[4,256,4096]{2,1,0:T(8,128)(2,1)} %convolution_convert_fusion), kind=kLoop, calls=%fused_computation | loop fusion | flops 7340032 | bytes 12582912 | tf_op jit(solution)/shard_map/reduce_sum | solution.py:50
  324.6 7.1 %clamp_convert_fusion = (bf16[256,4096]{1,0:T(8,128)(2,1)}, bf16[256,4096]{1,0:T(8,128)(2,1)}) fusion(bf16[256,4096]{1,0:T(8,128)(2,1)} %param.8, f32[256,4096]{1,0:T(8,128)} %convert_reduce_fusion, bf16[256,4096]{1,0:T(8,128)(2,1)} %param.9), kind=kLoop, calls=%fused_computation.4 | loop fusion | flops 11534336 | bytes 12582912 | tf_op jit(solution)/shard_map/convert_element_type | solution.py:25
  (2 shorter events, 0.0 us)
Async XLA Ops:
  7.2 133.7 %copy-start = (bf16[256,4096]{1,0:T(8,128)(2,1)S(1)}, bf16[256,4096]{1,0:T(8,128)(2,1)}, u32[]{:S(2)}) copy-start(bf16[256,4096]{1,0:T(8,128)(2,1)} %param.7) | copy-start | bytes 6291460
  7.2 133.7 %all-gather.2.cloned.1.call-start = ((), (), s32[]{:S(2)}) async-start(), calls=%async_computation | async-start | bytes 16842752 | tf_op jit(solution)/shard_map/all_gather | solution.py:30
  7.9 217.3 %copy-start.1 = (s32[2048]{0:T(1024)S(1)}, s32[2048]{0:T(1024)}, u32[]{:S(2)}) copy-start(s32[2048]{0:T(1024)} %param.10) | copy-start | bytes 24580
  150.8 151.4 %copy-start.2 = (s32[2048]{0:T(1024)S(1)}, s32[2048]{0:T(1024)}, u32[]{:S(2)}) copy-start(s32[2048]{0:T(1024)} %param.11) | copy-start | bytes 24580
Sparse Core Ops, SparseCore 0:
  11.7 129.1 all-gather.1
where the time goes:
time: 340 us
  blocking collectives  148 us (44%)
  waiting for transfers between devices  134 us (39%)
  matrix products  22.5 us (7%)
  other arithmetic  19.5 us (6%)
  between operations  15.9 us (5%)
    all_gather x1, waiting for transfers between devices, shards(): every_row = lax.all_gather(features, ('dp', 'vocab'), axis=0, tiled=True)  133 us
    pmax x1, blocking collectives, shards(): top_all = lax.pmax(highest, ('dp', 'vocab'))  74.4 us
    psum x1, blocking collectives, shards(): lax.psum((row_total * jnp.exp(highest - top_all), picked), ('dp', 'vocab'))  73.8 us
    dot_general x1, matrix products, shards(): lax.dot_general(signal_groups, row_groups, (((1,), (1,)), ((0,), (0,))),...  12.6 us
    dot_general x1, matrix products, shards(): lax.dot_general(every_row, head, (((1,), (1,)), ((), ())), preferred_elem...  9.85 us
    reduce_sum x1, other arithmetic, shards(): gradient = jnp.sum(rounded, axis=0)  7.29 us
    convert_element_type x1, other arithmetic, sophia_tail(): return (fresh.astype(jnp.bfloat16), clipped.astype(jnp.bfloat16))  7.12 us
  transfers between devices with their start and end apart: 1, of which 1 were waited for; matrix products, arithmetic and copies ran while one was open for 0% of the time, Pallas kernels for 0%

commit v1 on v0

--- a/solution.py
+++ b/solution.py
@@ -1,3 +1,4 @@
+import functools
 import jax
 import jax.numpy as jnp
 from jax import lax
@@ -5,6 +6,15 @@
 
 hess_decay = 0.99
 clip_scale = 0.05
+
+
+def feed_the_meshes(v0, mesh_ax, bus_axis):
+    for dev_i in (mesh_ax, bus_axis):
+        v0 = lax.psum(v0, dev_i)
+    return v0
+
+
+_review_tables = functools.partial(feed_the_meshes, mesh_ax="vocab", bus_axis="dp")
 
 
 def local_stats(logits, columns, labels):
@@ -35,7 +45,7 @@
     columns = own_offset + jnp.arange(voc_dev, dtype=jnp.int32)
     highest, row_total, picked = local_stats(logits, columns, true_labels)
     top_all = lax.pmax(highest, ("dp", "vocab"))
-    row_total, picked = lax.psum((row_total * jnp.exp(highest - top_all), picked), ("dp", "vocab"))
+    row_total, picked = _review_tables((row_total * jnp.exp(highest - top_all), picked))
     highest = top_all
     log_norm = highest + jnp.log(row_total)
     mean_loss = jnp.mean(log_norm - picked)

time: 340 us -> 528 us (1.55); the launches traced: 340 us -> 521 us
  blocking collectives: 148 us -> 329 us
    psum x1 -> x2, blocking collectives: 73.8 us -> 255 us  [feed_the_meshes(): v0 = lax.psum(v0, dev_i)]
where the time goes in v1:
time: 528 us; the launch traced here: 521 us
  blocking collectives  329 us (62%)
  waiting for transfers between devices  134 us (25%)
  matrix products  22.5 us (4%)
  other arithmetic  19.5 us (4%)
  between operations  15.9 us (3%)
    psum x2, blocking collectives, feed_the_meshes(): v0 = lax.psum(v0, dev_i)  255 us
    all_gather x1, waiting for transfers between devices, shards(): every_row = lax.all_gather(features, ('dp', 'vocab'), axis=0, tiled=True)  133 us
    pmax x1, blocking collectives, shards(): top_all = lax.pmax(highest, ('dp', 'vocab'))  74.4 us
    dot_general x1, matrix products, shards(): lax.dot_general(signal_groups, row_groups, (((1,), (1,)), ((0,), (0,))),...  12.6 us
  transfers between devices with their start and end apart: 1, of which 1 were waited for; matrix products, arithmetic and copies ran while one was open for 0% of the time, Pallas kernels for 0%

profile of v1, /device:TPU:1, one launch (start us, length us, event | category | flops | bytes accessed | tf_op | source)
XLA Modules:
  0.0 520.5 jit_solution(6046948159408463144)
XLA Ops:
  7.2 0.0 copy-start
  7.2 0.0 all-gather.2.cloned.1.call-start
  7.2 0.7 all-gather.2.cloned.1.call-update
  7.9 0.0 copy-start.1
  7.9 133.0 %all-gather.2.cloned.1.call-done = bf16[2048,4096]{1,0:T(8,128)(2,1)} async-done(((bf16[8,4096]{1,0:T(8,128)(2,1)}), bf16[2048,4096]{1,0:T(8,128)(2,1)}) %all-gather.2.cloned.1.call-update) | async-done | bytes 16777232 | tf_op jit(solution)/shard_map/all_gather | solution.py:40
  140.9 0.0 copy-done
  140.9 9.8 %fusion.2 = (f32[2048]{0:T(1024)S(1)}, f32[2048,256]{1,0:T(8,128)}) fusion(bf16[2048,4096]{1,0:T(8,128)(2,1)} %all-gather.2.cloned.1.call-done, bf16[256,4096]{1,0:T(8,128)(2,1)S(1)} %copy-done), kind=kOutput, calls=%fused_computation.13 | convolution fusion | flops 4295489536 | bytes 20979712 | tf_op jit(solution)/shard_map/dot_general | solution.py:41
  150.8 0.0 copy-start.2
  150.8 74.4 %pmax.7 = f32[2048]{0:T(1024)S(1)} all-reduce(f32[2048]{0:T(1024)S(1)} %get-tuple-element.13), channel_id=1, replica_groups=mesh['dp'=4,'vocab'=64] {'dp','vocab'}, use_global_device_ids=true, to_apply=%region_1.0 | all-reduce | flops 2048 | bytes 16384 | tf_op jit(solution)/shard_map/pmax | solution.py:47
  225.2 0.0 copy-done.1
  225.2 2.5 select_reduce_fusion
  227.7 243.8 %all-reduce = (f32[2048]{0:T(1024)S(1)}, f32[2048]{0:T(1024)S(1)}) all-reduce(f32[2048]{0:T(1024)S(1)} %exponential_multiply_fusion, f32[2048]{0:T(1024)S(1)} %get-tuple-element.3), channel_id=1, replica_groups=mesh['dp'=4,'vocab'=64] {'vocab'}, use_global_device_ids=true, to_apply=%region_3.4 | all-reduce | flops 4096 | bytes 32768 | tf_op jit(solution)/shard_map/psum | solution.py:13
  471.5 10.8 %all-reduce.1 = (f32[2048]{0:T(1024)S(1)}, f32[2048]{0:T(1024)S(1)}) all-reduce(f32[2048]{0:T(1024)S(1)} %get-tuple-element.5, f32[2048]{0:T(1024)S(1)} %get-tuple-element.6), channel_id=1, replica_groups=mesh['dp'=4,'vocab'=64] {'dp'}, use_global_device_ids=true, to_apply=%region_4.5 | all-reduce | flops 4096 | bytes 32768 | tf_op jit(solution)/shard_map/psum | solution.py:13
  482.3 0.6 subtract_reduce_fusion
  482.9 0.0 copy-done.2
  482.9 1.9 subtract_convert_fusion
  484.9 12.6 %convolution_convert_fusion = bf16[4,256,4096]{2,1,0:T(8,128)(2,1)} fusion(bf16[4,512,256]{2,1,0:T(8,128)(2,1)S(1)} %bitcast.7, bf16[4,512,4096]{2,1,0:T(8,128)(2,1)} %bitcast.6), kind=kOutput, calls=%fused_computation.1 | convolution fusion | flops 4299161600 | bytes 26214400 | tf_op jit(solution)/shard_map/dot_general | solution.py:56
  497.5 7.3 %convert_reduce_fusion = f32[256,4096]{1,0:T(8,128)} fusion(bf16[4,256,4096]{2,1,0:T(8,128)(2,1)} %convolution_convert_fusion), kind=kLoop, calls=%fused_computation | loop fusion | flops 7340032 | bytes 12582912 | tf_op jit(solution)/shard_map/reduce_sum | solution.py:60
  505.4 7.1 %clamp_convert_fusion = (bf16[256,4096]{1,0:T(8,128)(2,1)}, bf16[256,4096]{1,0:T(8,128)(2,1)}) fusion(bf16[256,4096]{1,0:T(8,128)(2,1)} %param.8, f32[256,4096]{1,0:T(8,128)} %convert_reduce_fusion, bf16[256,4096]{1,0:T(8,128)(2,1)} %param.9), kind=kLoop, calls=%fused_computation.4 | loop fusion | flops 11534336 | bytes 12582912 | tf_op jit(solution)/shard_map/convert_element_type | solution.py:35
  (2 shorter events, 0.0 us)
Async XLA Ops:
  7.2 133.7 %copy-start = (bf16[256,4096]{1,0:T(8,128)(2,1)S(1)}, bf16[256,4096]{1,0:T(8,128)(2,1)}, u32[]{:S(2)}) copy-start(bf16[256,4096]{1,0:T(8,128)(2,1)} %param.7) | copy-start | bytes 6291460
  7.2 133.7 %all-gather.2.cloned.1.call-start = ((), (), s32[]{:S(2)}) async-start(), calls=%async_computation | async-start | bytes 16842752 | tf_op jit(solution)/shard_map/all_gather | solution.py:40
  7.9 217.2 %copy-start.1 = (s32[2048]{0:T(1024)S(1)}, s32[2048]{0:T(1024)}, u32[]{:S(2)}) copy-start(s32[2048]{0:T(1024)} %param.10) | copy-start | bytes 24580
  150.8 332.2 %copy-start.2 = (s32[2048]{0:T(1024)S(1)}, s32[2048]{0:T(1024)}, u32[]{:S(2)}) copy-start(s32[2048]{0:T(1024)} %param.11) | copy-start | bytes 24580
Sparse Core Ops, SparseCore 0:
  11.7 129.1 all-gather.1

commit v2 on v0

--- a/solution.py
+++ b/solution.py
@@ -27,7 +27,15 @@
 
 def shards(features, head, momentum, hessian, true_labels, sampled_labels):
     voc_dev = head.shape[0]
-    every_row = lax.all_gather(features, ("dp", "vocab"), axis=0, tiled=True)
+    every_row = jnp.concatenate(
+        jax.lax.all_to_all(
+            jnp.stack([features] * jax.lax.psum(1, axis_name=("dp", "vocab")), 0),
+            axis_name=("dp", "vocab"),
+            split_axis=0,
+            concat_axis=0,
+        ),
+        0,
+    )
     logits = lax.dot_general(
         every_row, head, (((1,), (1,)), ((), ())), preferred_element_type=jnp.float32
     )

time: 340 us -> 583 us (1.71)
  waiting for transfers between devices: 134 us -> 368 us
  starting transfers between devices: 0.04 us -> 16.7 us
  between operations: 15.9 us -> 2.49 us
  local copies, waits for them, and re-layouts: 0.02 us -> 6.81 us
    all_to_all x0 -> x1, waiting for transfers between devices: none -> 368 us  [shards(): jax.lax.all_to_all(jnp.stack([features] * jax.lax.psum(1, axis_name=('dp'...]
    all_gather x1 -> x0, waiting for transfers between devices: 133 us -> none  [shards(): every_row = lax.all_gather(features, ('dp', 'vocab'), axis=0, tiled=True)]
    all_to_all x0 -> x1, starting transfers between devices: none -> 16.7 us  [shards(): jax.lax.all_to_all(jnp.stack([features] * jax.lax.psum(1, axis_name=('dp'...]
    another operation x0 -> x1, local copies, waits for them, and re-layouts: none -> 6.79 us  [shards(): jnp.stack([features] * jax.lax.psum(1, axis_name=('dp', 'vocab')), 0)]
where the time goes in v2:
time: 583 us
  waiting for transfers between devices  368 us (63%)
  blocking collectives  147 us (25%)
  matrix products  22.5 us (4%)
  other arithmetic  19.5 us (3%)
  starting transfers between devices  16.7 us (3%)
  local copies, waits for them, and re-layouts  6.81 us (1%)
    all_to_all x1, waiting for transfers between devices, shards(): jax.lax.all_to_all(jnp.stack([features] * jax.lax.psum(1, axis_name=('dp'...  368 us
    psum x1, blocking collectives, shards(): lax.psum((row_total * jnp.exp(highest - top_all), picked), ('dp', 'vocab'))  74.6 us
    pmax x1, blocking collectives, shards(): top_all = lax.pmax(highest, ('dp', 'vocab'))  72.2 us
    all_to_all x1, starting transfers between devices, shards(): jax.lax.all_to_all(jnp.stack([features] * jax.lax.psum(1, axis_name=('dp'...  16.7 us
    dot_general x1, matrix products, shards(): lax.dot_general(signal_groups, row_groups, (((1,), (1,)), ((0,), (0,))),...  12.6 us
  transfers between devices with their start and end apart: 1, of which 1 were waited for; matrix products, arithmetic and copies ran while one was open for 0% of the time, Pallas kernels for 0%

profile of v2, /device:TPU:1, one launch (start us, length us, event | category | flops | bytes accessed | tf_op | source)
XLA Modules:
  0.0 582.6 jit_solution(14914979208728636641)
XLA Ops:
  0.6 0.0 copy-start
  0.6 6.8 %stack.2 = bf16[256,8,4096]{2,1,0:T(8,128)(2,1)} broadcast(bf16[8,4096]{1,0:T(8,128)(2,1)} %param.6), dimensions={1,2} | broadcast | bytes 16842752 | tf_op jit(solution)/shard_map/stack | solution.py:32
  7.4 16.7 %all-to-all-start = ((bf16[256,8,4096]{2,1,0:T(8,128)(2,1)}), bf16[256,8,4096]{2,1,0:T(8,128)(2,1)}, u32[]{:S(2)}, u32[]{:S(2)}) async-start(bf16[256,8,4096]{2,1,0:T(8,128)(2,1)} %stack.2), calls=%async_computation | async-start | bytes 33554432 | tf_op jit(solution)/shard_map/all_to_all | solution.py:31
  24.1 0.0 copy-start.1
  24.1 0.0 copy-start.2
  24.1 367.9 %all-to-all-done = bf16[256,8,4096]{2,1,0:T(8,128)(2,1)} async-done(((bf16[256,8,4096]{2,1,0:T(8,128)(2,1)}), bf16[256,8,4096]{2,1,0:T(8,128)(2,1)}, u32[]{:S(2)}, u32[]{:S(2)}) %all-to-all-start) | async-done | bytes 16777248 | tf_op jit(solution)/shard_map/all_to_all | solution.py:31
  392.0 0.0 copy-done
  392.0 9.8 %fusion.4 = (f32[2048]{0:T(1024)S(1)}, f32[2048,256]{1,0:T(8,128)}) fusion(bf16[256,4096]{1,0:T(8,128)(2,1)S(1)} %copy-done, bf16[256,8,4096]{2,1,0:T(8,128)(2,1)} %all-to-all-done), kind=kOutput, calls=%fused_computation.15 | convolution fusion | flops 4295489536 | bytes 20979712 | tf_op jit(solution)/shard_map/dot_general | solution.py:39
  401.9 72.2 %pmax.7 = f32[2048]{0:T(1024)S(1)} all-reduce(f32[2048]{0:T(1024)S(1)} %get-tuple-element.11), channel_id=1, replica_groups=mesh['dp'=4,'vocab'=64] {'dp','vocab'}, use_global_device_ids=true, to_apply=%region_1.0 | all-reduce | flops 2048 | bytes 16384 | tf_op jit(solution)/shard_map/pmax | solution.py:45
  474.1 0.0 copy-done.1
  474.1 2.5 select_reduce_fusion
  476.6 74.6 %all-reduce = (f32[2048]{0:T(1024)S(1)}, f32[2048]{0:T(1024)S(1)}) all-reduce(f32[2048]{0:T(1024)S(1)} %exponential_multiply_fusion, f32[2048]{0:T(1024)S(1)} %get-tuple-element.3), channel_id=1, replica_groups=mesh['dp'=4,'vocab'=64] {'dp','vocab'}, use_global_device_ids=true, to_apply=%region_3.4 | all-reduce | flops 4096 | bytes 32768 | tf_op jit(solution)/shard_map/psum | solution.py:46
  551.2 0.6 subtract_reduce_fusion
  551.8 0.0 copy-done.2
  551.8 1.9 subtract_convert_fusion
  553.7 12.6 %convolution_convert_fusion = bf16[4,256,4096]{2,1,0:T(8,128)(2,1)} fusion(bf16[4,512,256]{2,1,0:T(8,128)(2,1)S(1)} %bitcast.10, bf16[4,512,4096]{2,1,0:T(8,128)(2,1)} %bitcast.2), kind=kOutput, calls=%fused_computation.3 | convolution fusion | flops 4299161600 | bytes 26214400 | tf_op jit(solution)/shard_map/dot_general | solution.py:54
  566.4 7.3 %convert_reduce_fusion = f32[256,4096]{1,0:T(8,128)} fusion(bf16[4,256,4096]{2,1,0:T(8,128)(2,1)} %convolution_convert_fusion), kind=kLoop, calls=%fused_computation.2 | loop fusion | flops 7340032 | bytes 12582912 | tf_op jit(solution)/shard_map/reduce_sum | solution.py:58
  574.3 7.1 %clamp_convert_fusion = (bf16[256,4096]{1,0:T(8,128)(2,1)}, bf16[256,4096]{1,0:T(8,128)(2,1)}) fusion(bf16[256,4096]{1,0:T(8,128)(2,1)} %param.8, f32[256,4096]{1,0:T(8,128)} %convert_reduce_fusion, bf16[256,4096]{1,0:T(8,128)(2,1)} %param.9), kind=kLoop, calls=%fused_computation.6 | loop fusion | flops 11534336 | bytes 12582912 | tf_op jit(solution)/shard_map/convert_element_type | solution.py:25
  (2 shorter events, 0.0 us)
Async XLA Ops:
  0.6 391.4 %copy-start = (bf16[256,4096]{1,0:T(8,128)(2,1)S(1)}, bf16[256,4096]{1,0:T(8,128)(2,1)}, u32[]{:S(2)}) copy-start(bf16[256,4096]{1,0:T(8,128)(2,1)} %param.7) | copy-start | bytes 6291460
  7.4 384.6 %all-to-all-start = ((bf16[256,8,4096]{2,1,0:T(8,128)(2,1)}), bf16[256,8,4096]{2,1,0:T(8,128)(2,1)}, u32[]{:S(2)}, u32[]{:S(2)}) async-start(bf16[256,8,4096]{2,1,0:T(8,128)(2,1)} %stack.2), calls=%async_computation | async-start | bytes 33554432 | tf_op jit(solution)/shard_map/all_to_all | solution.py:31
  24.1 449.9 %copy-start.1 = (s32[2048]{0:T(1024)S(1)}, s32[2048]{0:T(1024)}, u32[]{:S(2)}) copy-start(s32[2048]{0:T(1024)} %param.10) | copy-start | bytes 24580
  24.1 527.7 %copy-start.2 = (s32[2048]{0:T(1024)S(1)}, s32[2048]{0:T(1024)}, u32[]{:S(2)}) copy-start(s32[2048]{0:T(1024)} %param.11) | copy-start | bytes 24580
